TPU v7x, 128 devices: a whole 4x4x4 slice. The times are simulated.
128 devices in a mesh: tm: 16 (over z_lo, x, core), rows: 8 (over y, z_hi).
Axes of the slice: x: 4, y: 4, z: 4 (z_hi: 2, z_lo: 2; z = z_hi * 2 + z_lo), core: 2. Of those that a mesh axis runs over, the one named last changes fastest.
Arguments:
- latents: bfloat16 [16, 96, 160, 384], P('tm', 'rows'), may hold values from -6 to 6
- norm_gain_one: float32 [384], replicated, may hold values from 0.5 to 2
- conv_weight_one: bfloat16 [10368, 384], replicated, may hold values from -0.0625 to 0.0625
- conv_bias_one: float32 [384], replicated, may hold values from -3 to 3
- norm_gain_two: float32 [384], replicated, may hold values from 0.5 to 2
- conv_weight_two: bfloat16 [10368, 384], replicated, may hold values from -0.0625 to 0.0625
- conv_bias_two: float32 [384], replicated, may hold values from -3 to 3
Outputs:
- block_out: bfloat16 [16, 96, 160, 384], P('tm', 'rows')
All inputs are finite; a program needn't handle non-finite values.
Results may differ from a plain program's by a relative error of at most 0.0041.
Values may be sent and summed in bfloat16 or wider, within the bound.
A program may use at most 128 MiB of HBM per device.

v0:
```python
import jax
import jax.numpy as jnp
from jax import lax
from jax.sharding import PartitionSpec as P


def shifted(block, axis, distance):
    devices = range(lax.axis_size(axis))
    route = [(i - distance, i) for i in devices if i - distance in devices]
    return lax.ppermute(block, axis, route)


def padded(block, sides, width):
    for axis, dim in sides:
        count = lax.axis_size(axis)
        forward = [(i, i + 1) for i in range(count - 1)]
        backward = [(target, source) for source, target in forward]
        low = lax.ppermute(
            lax.slice_in_dim(block, block.shape[dim] - width, None, axis=dim), axis, forward
        )
        high = lax.ppermute(lax.slice_in_dim(block, 0, width, axis=dim), axis, backward)
        block = jnp.concatenate([low, block, high], axis=dim)
    return block


def norm_act(values, gain):
    wide = values.astype(jnp.float32)
    scaled = wide * lax.rsqrt(jnp.mean(wide * wide, axis=-1, keepdims=True) + 1e-06) * gain
    return jax.nn.silu(scaled)


def convolve_frame(extended, weight):
    height = extended.shape[1] - 2
    width = extended.shape[2] - 2
    channels = extended.shape[3]
    taps = weight.reshape(3, 3, 3 * channels, channels)
    total = jnp.zeros((height * width, channels), jnp.float32)
    for frame_tap in range(3):
        for row_tap in range(3):
            window = extended[frame_tap, row_tap : row_tap + height]
            joined = jnp.concatenate(
                [window[:, col_tap : col_tap + width] for col_tap in range(3)], axis=-1
            )
            total = total + jnp.dot(
                joined.reshape(height * width, 3 * channels),
                taps[frame_tap, row_tap],
                preferred_element_type=jnp.float32,
            )
    return total.reshape(height, width, channels)


def earlier_frames(block):
    previous = shifted(block, "tm", 1)
    before = shifted(block, "tm", 2)
    return jnp.concatenate([before, previous], axis=0)


def extend(field):
    stacked = jnp.concatenate([earlier_frames(field), field], axis=0)
    stacked = padded(stacked, (("rows", 1),), 1)
    return jnp.pad(stacked, ((0, 0), (0, 0), (1, 1), (0, 0)))


def convolve(field, weight, bias):
    result = convolve_frame(extend(field), weight) + bias
    return result[None]


def on_device(
    latents,
    norm_gain_one,
    conv_weight_one,
    conv_bias_one,
    norm_gain_two,
    conv_weight_two,
    conv_bias_two,
):
    first = norm_act(latents, norm_gain_one).astype(jnp.bfloat16)
    middle = convolve(first, conv_weight_one, conv_bias_one)
    second = norm_act(middle, norm_gain_two).astype(jnp.bfloat16)
    result = convolve(second, conv_weight_two, conv_bias_two) + latents.astype(jnp.float32)
    return result.astype(jnp.bfloat16)


def solution(mesh):
    return jax.shard_map(
        on_device,
        mesh=mesh,
        in_specs=(P("tm", "rows", None, None), P(), P(), P(), P(), P(), P()),
        out_specs=P("tm", "rows", None, None),
        check_vma=False,
    )
```

profile of v0, /device:TPU:31, one launch (start us, length us, event | category | flops | bytes accessed | tf_op | source)
XLA Modules:
  0.0 285.8 jit_solution(17276484480525710919)
XLA Ops:
  0.0 1.9 fusion.15
  1.9 2.3 fusion.22
  4.2 3.5 %collective-permute-start = (bf16[1,12,160,384]{3,2,1,0:T(8,128)(2,1)S(1)}, bf16[1,12,160,384]{3,2,1,0:T(8,128)(2,1)S(1)}, u32[]{:S(2)}, u32[]{:S(2)}) collective-permute-start(bf16[1,12,160,384]{3,2,1,0:T(8,128)(2,1)S(1)} %fusion.22), channel_id=1, source_target_pairs={{0,16},{8,24},{16,32},{24,40},{32,48},{40,56},{48,64},{56,72},{64,... | collective-permute-start | bytes 4423688 | tf_op jit(solution)/shard_map/ppermute | solution.py:10
  7.7 4.0 %collective-permute-start.1 = (bf16[1,12,160,384]{3,2,1,0:T(8,128)(2,1)S(1)}, bf16[1,12,160,384]{3,2,1,0:T(8,128)(2,1)S(1)}, u32[]{:S(2)}, u32[]{:S(2)}) collective-permute-start(bf16[1,12,160,384]{3,2,1,0:T(8,128)(2,1)S(1)} %fusion.22), channel_id=1, source_target_pairs={{0,8},{8,16},{16,24},{24,32},{32,40},{40,48},{48,56},{56,64},{64,7... | collective-permute-start | bytes 4423688 | tf_op jit(solution)/shard_map/ppermute | solution.py:10
  11.6 27.6 %collective-permute-done = bf16[1,12,160,384]{3,2,1,0:T(8,128)(2,1)S(1)} collective-permute-done((bf16[1,12,160,384]{3,2,1,0:T(8,128)(2,1)S(1)}, bf16[1,12,160,384]{3,2,1,0:T(8,128)(2,1)S(1)}, u32[]{:S(2)}, u32[]{:S(2)}) %collective-permute-start) | collective-permute-done | bytes 1474592 | tf_op jit(solution)/shard_map/ppermute | solution.py:10
  39.2 16.3 %collective-permute-done.1 = bf16[1,12,160,384]{3,2,1,0:T(8,128)(2,1)S(1)} collective-permute-done((bf16[1,12,160,384]{3,2,1,0:T(8,128)(2,1)S(1)}, bf16[1,12,160,384]{3,2,1,0:T(8,128)(2,1)S(1)}, u32[]{:S(2)}, u32[]{:S(2)}) %collective-permute-start.1) | collective-permute-done | bytes 1474592 | tf_op jit(solution)/shard_map/ppermute | solution.py:10
  55.7 10.3 %collective-permute-start.2 = (bf16[3,1,160,384]{3,2,1,0:T(8,128)(2,1)S(1)}, bf16[3,1,160,384]{3,2,1,0:T(8,128)(2,1)S(1)}, u32[]{:S(2)}, u32[]{:S(2)}) collective-permute-start(bf16[3,1,160,384]{3,2,1,0:T(8,128)(2,1)S(1)} %get-tuple-element.25), channel_id=1, source_target_pairs={{0,1},{1,2},{2,3},{3,4},{4,5},{5,6},{6,7},{8,9},{9,10},{10,11},{11... | collective-permute-start | bytes 1105928 | tf_op jit(solution)/shard_map/ppermute | solution.py:18
  66.0 2.3 collective-permute-start.3
  68.3 3.6 %collective-permute-done.2 = bf16[3,1,160,384]{3,2,1,0:T(8,128)(2,1)S(1)} collective-permute-done((bf16[3,1,160,384]{3,2,1,0:T(8,128)(2,1)S(1)}, bf16[3,1,160,384]{3,2,1,0:T(8,128)(2,1)S(1)}, u32[]{:S(2)}, u32[]{:S(2)}) %collective-permute-start.2) | collective-permute-done | bytes 368672 | tf_op jit(solution)/shard_map/ppermute | solution.py:18
  71.9 8.0 %collective-permute-done.3 = bf16[3,1,160,384]{3,2,1,0:T(8,128)(2,1)S(1)} collective-permute-done((bf16[3,1,160,384]{3,2,1,0:T(8,128)(2,1)S(1)}, bf16[3,1,160,384]{3,2,1,0:T(8,128)(2,1)S(1)}, u32[]{:S(2)}, u32[]{:S(2)}) %collective-permute-start.3) | collective-permute-done | bytes 368672 | tf_op jit(solution)/shard_map/ppermute | solution.py:21
  79.9 2.6 fusion.10
  82.4 1.5 slice_bitcast_fusion.9
  83.9 1.6 fusion.51
  86.0 3.8 %fusion.39 = f32[1920,384]{1,0:T(8,128)S(1)} fusion(bf16[1920,1152]{1,0:T(8,128)(2,1)S(1)} %bitcast.136, bf16[3,3,1152,384]{3,2,1,0:T(8,128)(2,1)} %bitcast.152), kind=kOutput, calls=%fused_computation.104 | convolution fusion | flops 1698693120 | bytes 8257536 | tf_op jit(solution)/shard_map/dot_general | solution.py:44
  90.3 3.8 %fusion.37 = f32[1920,384]{1,0:T(8,128)S(1)} fusion(bf16[1920,1152]{1,0:T(8,128)(2,1)S(1)} %bitcast.137, bf16[3,3,1152,384]{3,2,1,0:T(8,128)(2,1)} %bitcast.153), kind=kOutput, calls=%fused_computation.100 | convolution fusion | flops 1698693120 | bytes 8257536 | tf_op jit(solution)/shard_map/dot_general | solution.py:44
  94.1 1.6 fusion.49
  96.3 5.4 %fusion.38 = f32[1920,384]{1,0:T(8,128)} fusion(bf16[1920,1152]{1,0:T(8,128)(2,1)S(1)} %bitcast.138, bf16[3,3,1152,384]{3,2,1,0:T(8,128)(2,1)} %bitcast.154), kind=kOutput, calls=%fused_computation.102 | convolution fusion | flops 1698693120 | bytes 8257536 | tf_op jit(solution)/shard_map/dot_general | solution.py:44
  101.6 1.8 fusion.53
  104.0 5.4 %fusion.36 = f32[1920,384]{1,0:T(8,128)} fusion(bf16[1920,1152]{1,0:T(8,128)(2,1)S(1)} %bitcast.139, bf16[3,3,1152,384]{3,2,1,0:T(8,128)(2,1)} %bitcast.155), kind=kOutput, calls=%fused_computation.98 | convolution fusion | flops 1698693120 | bytes 8257536 | tf_op jit(solution)/shard_map/dot_general | solution.py:44
  109.8 5.4 %fusion.35 = f32[1920,384]{1,0:T(8,128)} fusion(bf16[1920,1152]{1,0:T(8,128)(2,1)S(1)} %bitcast.140, bf16[3,3,1152,384]{3,2,1,0:T(8,128)(2,1)} %bitcast.156), kind=kOutput, calls=%fused_computation.96 | convolution fusion | flops 1698693120 | bytes 8257536 | tf_op jit(solution)/shard_map/dot_general | solution.py:44
  115.2 1.6 fusion.55
  117.3 5.4 %fusion.34 = f32[1920,384]{1,0:T(8,128)} fusion(bf16[1920,1152]{1,0:T(8,128)(2,1)S(1)} %bitcast.141, bf16[3,3,1152,384]{3,2,1,0:T(8,128)(2,1)} %bitcast.157), kind=kOutput, calls=%fused_computation.94 | convolution fusion | flops 1698693120 | bytes 8257536 | tf_op jit(solution)/shard_map/dot_general | solution.py:44
  123.7 5.4 %fusion.33 = f32[1920,384]{1,0:T(8,128)} fusion(bf16[1920,1152]{1,0:T(8,128)(2,1)S(1)} %bitcast.142, bf16[3,3,1152,384]{3,2,1,0:T(8,128)(2,1)} %bitcast.158), kind=kOutput, calls=%fused_computation.92 | convolution fusion | flops 1698693120 | bytes 8257536 | tf_op jit(solution)/shard_map/dot_general | solution.py:44
  130.3 5.4 %fusion.32 = f32[1920,384]{1,0:T(8,128)} fusion(bf16[1920,1152]{1,0:T(8,128)(2,1)S(1)} %bitcast.143, bf16[3,3,1152,384]{3,2,1,0:T(8,128)(2,1)} %bitcast.159), kind=kOutput, calls=%fused_computation.90 | convolution fusion | flops 1698693120 | bytes 8257536 | tf_op jit(solution)/shard_map/dot_general | solution.py:44
  136.1 1.4 copy-done.1
  137.5 0.9 copy-done.2
  138.4 9.0 %multiply_reduce_fusion = (f32[1920]{0:T(1024)S(1)}, f32[1920,384]{1,0:T(8,128)S(1)}) fusion(f32[384]{0:T(512)S(1)} %copy-done.3, bf16[1920,1152]{1,0:T(8,128)(2,1)S(1)} %bitcast.132, bf16[3,3,1152,384]{3,2,1,0:T(8,128)(2,1)} %bitcast.160, f32[1920,384]{1,0:T(8,128)} %fusion.32, f32[1920,384]{1,0:T(8,128)} %fusion.33, f32[1920,384]{1,0:T(8,128)} %fusion.34, ...), kind=kOutput, calls=%fused_computation.51 | convolution fusion | flops 1706801280 | bytes 31859712 | tf_op jit(solution)/shard_map/dot_general | solution.py:44
  147.5 0.9 multiply_convert_fusion
  148.5 1.9 collective-permute-start.4
  150.4 4.6 %collective-permute-start.5 = (bf16[1,12,160,384]{3,2,1,0:T(8,128)(2,1)S(1)}, bf16[1,12,160,384]{3,2,1,0:T(8,128)(2,1)S(1)}, u32[]{:S(2)}, u32[]{:S(2)}) collective-permute-start(bf16[1,12,160,384]{3,2,1,0:T(8,128)(2,1)S(1)} %multiply_convert_fusion), channel_id=1, source_target_pairs={{0,8},{8,16},{16,24},{24,32},{32,40},{40,48},{48,56},{56,64},{64,7... | collective-permute-start | bytes 4423688 | tf_op jit(solution)/shard_map/ppermute | solution.py:10
  155.0 28.8 %collective-permute-done.4 = bf16[1,12,160,384]{3,2,1,0:T(8,128)(2,1)S(1)} collective-permute-done((bf16[1,12,160,384]{3,2,1,0:T(8,128)(2,1)S(1)}, bf16[1,12,160,384]{3,2,1,0:T(8,128)(2,1)S(1)}, u32[]{:S(2)}, u32[]{:S(2)}) %collective-permute-start.4) | collective-permute-done | bytes 1474592 | tf_op jit(solution)/shard_map/ppermute | solution.py:10
  183.8 14.5 %collective-permute-done.5 = bf16[1,12,160,384]{3,2,1,0:T(8,128)(2,1)S(1)} collective-permute-done((bf16[1,12,160,384]{3,2,1,0:T(8,128)(2,1)S(1)}, bf16[1,12,160,384]{3,2,1,0:T(8,128)(2,1)S(1)}, u32[]{:S(2)}, u32[]{:S(2)}) %collective-permute-start.5) | collective-permute-done | bytes 1474592 | tf_op jit(solution)/shard_map/ppermute | solution.py:10
  198.4 5.3 %collective-permute-start.6 = (bf16[3,1,160,384]{3,2,1,0:T(8,128)(2,1)S(1)}, bf16[3,1,160,384]{3,2,1,0:T(8,128)(2,1)S(1)}, u32[]{:S(2)}, u32[]{:S(2)}) collective-permute-start(bf16[3,1,160,384]{3,2,1,0:T(8,128)(2,1)S(1)} %get-tuple-element.23), channel_id=1, source_target_pairs={{0,1},{1,2},{2,3},{3,4},{4,5},{5,6},{6,7},{8,9},{9,10},{10,11},{11... | collective-permute-start | bytes 1105928 | tf_op jit(solution)/shard_map/ppermute | solution.py:18
  203.7 5.9 %collective-permute-start.7 = (bf16[3,1,160,384]{3,2,1,0:T(8,128)(2,1)S(1)}, bf16[3,1,160,384]{3,2,1,0:T(8,128)(2,1)S(1)}, u32[]{:S(2)}, u32[]{:S(2)}) collective-permute-start(bf16[3,1,160,384]{3,2,1,0:T(8,128)(2,1)S(1)} %get-tuple-element.24), channel_id=1, source_target_pairs={{1,0},{2,1},{3,2},{4,3},{5,4},{6,5},{7,6},{9,8},{10,9},{11,10},{12... | collective-permute-start | bytes 1105928 | tf_op jit(solution)/shard_map/ppermute | solution.py:21
  209.7 6.4 %collective-permute-done.6 = bf16[3,1,160,384]{3,2,1,0:T(8,128)(2,1)S(1)} collective-permute-done((bf16[3,1,160,384]{3,2,1,0:T(8,128)(2,1)S(1)}, bf16[3,1,160,384]{3,2,1,0:T(8,128)(2,1)S(1)}, u32[]{:S(2)}, u32[]{:S(2)}) %collective-permute-start.6) | collective-permute-done | bytes 368672 | tf_op jit(solution)/shard_map/ppermute | solution.py:18
  216.1 8.1 %collective-permute-done.7 = bf16[3,1,160,384]{3,2,1,0:T(8,128)(2,1)S(1)} collective-permute-done((bf16[3,1,160,384]{3,2,1,0:T(8,128)(2,1)S(1)}, bf16[3,1,160,384]{3,2,1,0:T(8,128)(2,1)S(1)}, u32[]{:S(2)}, u32[]{:S(2)}) %collective-permute-start.7) | collective-permute-done | bytes 368672 | tf_op jit(solution)/shard_map/ppermute | solution.py:21
  224.2 2.8 select_maximum_fusion
  227.0 1.5 slice_bitcast_fusion
  231.3 3.8 %fusion.30 = f32[1920,384]{1,0:T(8,128)S(1)} fusion(bf16[1920,1152]{1,0:T(8,128)(2,1)S(1)} %bitcast.144, bf16[3,3,1152,384]{3,2,1,0:T(8,128)(2,1)} %bitcast.161), kind=kOutput, calls=%fused_computation.85 | convolution fusion | flops 1698693120 | bytes 8257536 | tf_op jit(solution)/shard_map/dot_general | solution.py:44
  235.5 3.7 %fusion.31 = f32[1920,384]{1,0:T(8,128)S(1)} fusion(bf16[1920,1152]{1,0:T(8,128)(2,1)S(1)} %bitcast.145, bf16[3,3,1152,384]{3,2,1,0:T(8,128)(2,1)} %bitcast.162), kind=kOutput, calls=%fused_computation.87 | convolution fusion | flops 1698693120 | bytes 8257536 | tf_op jit(solution)/shard_map/dot_general | solution.py:44
  240.8 3.8 %fusion.29 = f32[1920,384]{1,0:T(8,128)S(1)} fusion(bf16[1920,1152]{1,0:T(8,128)(2,1)S(1)} %bitcast.146, bf16[3,3,1152,384]{3,2,1,0:T(8,128)(2,1)} %bitcast.163), kind=kOutput, calls=%fused_computation.83 | convolution fusion | flops 1698693120 | bytes 8257536 | tf_op jit(solution)/shard_map/dot_general | solution.py:44
  245.7 3.8 %fusion.28 = f32[1920,384]{1,0:T(8,128)S(1)} fusion(bf16[1920,1152]{1,0:T(8,128)(2,1)S(1)} %bitcast.147, bf16[3,3,1152,384]{3,2,1,0:T(8,128)(2,1)} %bitcast.164), kind=kOutput, calls=%fused_computation.81 | convolution fusion | flops 1698693120 | bytes 8257536 | tf_op jit(solution)/shard_map/dot_general | solution.py:44
  250.7 5.3 %fusion.27 = f32[1920,384]{1,0:T(8,128)} fusion(bf16[1920,1152]{1,0:T(8,128)(2,1)S(1)} %bitcast.148, bf16[3,3,1152,384]{3,2,1,0:T(8,128)(2,1)} %bitcast.165), kind=kOutput, calls=%fused_computation.79 | convolution fusion | flops 1698693120 | bytes 8257536 | tf_op jit(solution)/shard_map/dot_general | solution.py:44
  257.5 5.5 %fusion.26 = f32[1920,384]{1,0:T(8,128)} fusion(bf16[1920,1152]{1,0:T(8,128)(2,1)S(1)} %bitcast.149, bf16[3,3,1152,384]{3,2,1,0:T(8,128)(2,1)} %bitcast.166), kind=kOutput, calls=%fused_computation.77 | convolution fusion | flops 1698693120 | bytes 8257536 | tf_op jit(solution)/shard_map/dot_general | solution.py:44
  264.2 5.4 %fusion.25 = f32[1920,384]{1,0:T(8,128)} fusion(bf16[1920,1152]{1,0:T(8,128)(2,1)S(1)} %bitcast.150, bf16[3,3,1152,384]{3,2,1,0:T(8,128)(2,1)} %bitcast.167), kind=kOutput, calls=%fused_computation.75 | convolution fusion | flops 1698693120 | bytes 8257536 | tf_op jit(solution)/shard_map/dot_general | solution.py:44
  270.8 5.4 %fusion.24 = f32[1920,384]{1,0:T(8,128)} fusion(bf16[1920,1152]{1,0:T(8,128)(2,1)S(1)} %bitcast.151, bf16[3,3,1152,384]{3,2,1,0:T(8,128)(2,1)} %bitcast.168), kind=kOutput, calls=%fused_computation.73 | convolution fusion | flops 1698693120 | bytes 8257536 | tf_op jit(solution)/shard_map/dot_general | solution.py:44
  276.7 7.3 %add_add_fusion = f32[1920,384]{1,0:T(8,128)S(1)} fusion(f32[1920,384]{1,0:T(8,128)} %fusion.24, f32[1920,384]{1,0:T(8,128)} %fusion.25, f32[1920,384]{1,0:T(8,128)} %fusion.26, f32[1920,384]{1,0:T(8,128)} %fusion.27, f32[1920,384]{1,0:T(8,128)S(1)} %fusion.28, f32[1920,384]{1,0:T(8,128)S(1)} %fusion.29, f32[1920,384]{1,0:T(8,128)S(1)} %fusion.31, ...), kind=kOutput, calls=%fused_computation.49 | convolution fusion | flops 1704591360 | bytes 31850496 | tf_op jit(solution)/shard_map/dot_general | solution.py:44
  284.0 1.5 fusion.23
  (43 shorter events, 17.0 us)
Async XLA Ops:
  4.2 35.0 %collective-permute-start = (bf16[1,12,160,384]{3,2,1,0:T(8,128)(2,1)S(1)}, bf16[1,12,160,384]{3,2,1,0:T(8,128)(2,1)S(1)}, u32[]{:S(2)}, u32[]{:S(2)}) collective-permute-start(bf16[1,12,160,384]{3,2,1,0:T(8,128)(2,1)S(1)} %fusion.22), channel_id=1, source_target_pairs={{0,16},{8,24},{16,32},{24,40},{32,48},{40,56},{48,64},{56,72},{64,... | collective-permute-start | bytes 4423688 | tf_op jit(solution)/shard_map/ppermute | solution.py:10
  7.7 47.9 %collective-permute-start.1 = (bf16[1,12,160,384]{3,2,1,0:T(8,128)(2,1)S(1)}, bf16[1,12,160,384]{3,2,1,0:T(8,128)(2,1)S(1)}, u32[]{:S(2)}, u32[]{:S(2)}) collective-permute-start(bf16[1,12,160,384]{3,2,1,0:T(8,128)(2,1)S(1)} %fusion.22), channel_id=1, source_target_pairs={{0,8},{8,16},{16,24},{24,32},{32,40},{40,48},{48,56},{56,64},{64,7... | collective-permute-start | bytes 4423688 | tf_op jit(solution)/shard_map/ppermute | solution.py:10
  55.7 16.2 %collective-permute-start.2 = (bf16[3,1,160,384]{3,2,1,0:T(8,128)(2,1)S(1)}, bf16[3,1,160,384]{3,2,1,0:T(8,128)(2,1)S(1)}, u32[]{:S(2)}, u32[]{:S(2)}) collective-permute-start(bf16[3,1,160,384]{3,2,1,0:T(8,128)(2,1)S(1)} %get-tuple-element.25), channel_id=1, source_target_pairs={{0,1},{1,2},{2,3},{3,4},{4,5},{5,6},{6,7},{8,9},{9,10},{10,11},{11... | collective-permute-start | bytes 1105928 | tf_op jit(solution)/shard_map/ppermute | solution.py:18
  66.0 13.9 %collective-permute-start.3 = (bf16[3,1,160,384]{3,2,1,0:T(8,128)(2,1)S(1)}, bf16[3,1,160,384]{3,2,1,0:T(8,128)(2,1)S(1)}, u32[]{:S(2)}, u32[]{:S(2)}) collective-permute-start(bf16[3,1,160,384]{3,2,1,0:T(8,128)(2,1)S(1)} %get-tuple-element.26), channel_id=1, source_target_pairs={{1,0},{2,1},{3,2},{4,3},{5,4},{6,5},{7,6},{9,8},{10,9},{11,10},{12... | collective-permute-start | bytes 1105928 | tf_op jit(solution)/shard_map/ppermute | solution.py:21
  135.7 1.8 copy-start.1
  135.7 2.7 copy-start.2
  135.7 2.7 copy-start.3
  138.4 9.1 %copy-start.4 = (f32[384]{0:T(512)S(1)}, f32[384]{0:T(512)}, u32[]{:S(2)}) copy-start(f32[384]{0:T(512)} %param.11) | copy-start | bytes 4612
  148.5 35.4 %collective-permute-start.4 = (bf16[1,12,160,384]{3,2,1,0:T(8,128)(2,1)S(1)}, bf16[1,12,160,384]{3,2,1,0:T(8,128)(2,1)S(1)}, u32[]{:S(2)}, u32[]{:S(2)}) collective-permute-start(bf16[1,12,160,384]{3,2,1,0:T(8,128)(2,1)S(1)} %multiply_convert_fusion), channel_id=1, source_target_pairs={{0,16},{8,24},{16,32},{24,40},{32,48},{40,56},{48,64},{56,72},{64,... | collective-permute-start | bytes 4423688 | tf_op jit(solution)/shard_map/ppermute | solution.py:10
  150.4 47.9 %collective-permute-start.5 = (bf16[1,12,160,384]{3,2,1,0:T(8,128)(2,1)S(1)}, bf16[1,12,160,384]{3,2,1,0:T(8,128)(2,1)S(1)}, u32[]{:S(2)}, u32[]{:S(2)}) collective-permute-start(bf16[1,12,160,384]{3,2,1,0:T(8,128)(2,1)S(1)} %multiply_convert_fusion), channel_id=1, source_target_pairs={{0,8},{8,16},{16,24},{24,32},{32,40},{40,48},{48,56},{56,64},{64,7... | collective-permute-start | bytes 4423688 | tf_op jit(solution)/shard_map/ppermute | solution.py:10
  198.4 17.7 %collective-permute-start.6 = (bf16[3,1,160,384]{3,2,1,0:T(8,128)(2,1)S(1)}, bf16[3,1,160,384]{3,2,1,0:T(8,128)(2,1)S(1)}, u32[]{:S(2)}, u32[]{:S(2)}) collective-permute-start(bf16[3,1,160,384]{3,2,1,0:T(8,128)(2,1)S(1)} %get-tuple-element.23), channel_id=1, source_target_pairs={{0,1},{1,2},{2,3},{3,4},{4,5},{5,6},{6,7},{8,9},{9,10},{10,11},{11... | collective-permute-start | bytes 1105928 | tf_op jit(solution)/shard_map/ppermute | solution.py:18
  203.7 20.4 %collective-permute-start.7 = (bf16[3,1,160,384]{3,2,1,0:T(8,128)(2,1)S(1)}, bf16[3,1,160,384]{3,2,1,0:T(8,128)(2,1)S(1)}, u32[]{:S(2)}, u32[]{:S(2)}) collective-permute-start(bf16[3,1,160,384]{3,2,1,0:T(8,128)(2,1)S(1)} %get-tuple-element.24), channel_id=1, source_target_pairs={{1,0},{2,1},{3,2},{4,3},{5,4},{6,5},{7,6},{9,8},{10,9},{11,10},{12... | collective-permute-start | bytes 1105928 | tf_op jit(solution)/shard_map/ppermute | solution.py:21
  276.7 7.3 %copy-start = (bf16[1,12,160,384]{3,2,1,0:T(8,128)(2,1)S(1)}, bf16[1,12,160,384]{3,2,1,0:T(8,128)(2,1)}, u32[]{:S(2)}) copy-start(bf16[1,12,160,384]{3,2,1,0:T(8,128)(2,1)} %param.7) | copy-start | bytes 4423684
  276.7 7.3 %copy-start.5 = (f32[384]{0:T(512)S(1)}, f32[384]{0:T(512)}, u32[]{:S(2)}) copy-start(f32[384]{0:T(512)} %param.13) | copy-start | bytes 4612
where the time goes:
time: 289 us; the launch traced here: 286 us
  waiting for transfers between devices  113 us (39%)
  matrix products  93 us (32%)
  starting transfers between devices  37.8 us (13%)
  other arithmetic  21.1 us (7%)
  local copies, waits for them, and re-layouts  19.8 us (7%)
    dot_general x18, matrix products, convolve_frame(): jnp.dot(joined.reshape(height * width, 3 * channels), taps[frame_tap, row...  93 us
    ppermute x4, waiting for transfers between devices, shifted(): return lax.ppermute(block, axis, route)  87.3 us
    ppermute x2, waiting for transfers between devices, padded(): lax.ppermute(lax.slice_in_dim(block, 0, width, axis=dim), axis, backward)  16.1 us
    ppermute x2, starting transfers between devices, padded(): lax.ppermute(lax.slice_in_dim(block, block.shape[dim] - width, None, axis...  15.6 us
    slice x14, local copies, waits for them, and re-layouts, convolve_frame(): window[:, col_tap:col_tap + width]  14.4 us
    ppermute x4, starting transfers between devices, shifted(): return lax.ppermute(block, axis, route)  14 us
    ppermute x2, waiting for transfers between devices, padded(): lax.ppermute(lax.slice_in_dim(block, block.shape[dim] - width, None, axis...  10 us
    concatenate x18, other arithmetic, convolve_frame(): jnp.concatenate([window[:, col_tap:col_tap + width] for col_tap in range(...  8.98 us
  transfers between devices with their start and end apart: 8, of which 8 were waited for; matrix products, arithmetic and copies ran while one was open for 0% of the time, Pallas kernels for 0%

commit v1 on v0

v1 whole, which is shorter than its diff:
```python
import functools

import jax
import jax.numpy as jnp
from jax import lax
from jax.experimental import pallas as pl
from jax.experimental.pallas import tpu as pltpu
from jax.sharding import PartitionSpec as P

MESH = pl.DeviceIdType.MESH
F32, BF16 = jnp.float32, jnp.bfloat16

C = 384
LANES = C // 128
H = 12
COLS = 160
N = 16
W = COLS // N
WH = W + 2
QI, RI = 3, 4
QO, RO = 4, 3
PI = RI * WH
PO = 32
PAIRS = 5


def norm_act(v, gain):
    scale = lax.rsqrt(jnp.mean(v * v, axis=-1, keepdims=True) + 1e-06)
    u = v * scale * gain
    return u / (1.0 + jnp.exp(-u))


def later(v, frames):
    at = lax.broadcasted_iota(jnp.int32, v.shape, v.ndim - 2)
    return jnp.where(at < frames, 0.0, pltpu.roll(v, frames, v.ndim - 2))


def peer(me, k):
    z, x, c = me // 8, (me // 2) % 4, me % 2
    dz, dx, dc = k // 8, (k // 2) % 4, k % 2
    return ((z + dz) % 2) * 8 + ((x + dx) % 4) * 2 + (c + dc) % 2


def source(me, k):
    z, x, c = me // 8, (me // 2) % 4, me % 2
    dz, dx, dc = k // 8, (k // 2) % 4, k % 2
    return ((z + dz) % 2) * 8 + ((x + 4 - dx) % 4) * 2 + (c + dc) % 2


ORDER = (12, 13, 4, 5, 10, 11, 14, 15, 2, 3, 6, 7, 8, 9, 1)


def kernel(
    lat, g1, w1, b1, g2, w2, b2,
    out,
    wc1, wc2, field, second, recv, send, nrm, pk, tr, prod, otr, ostage,
    w_sem, in_send, in_recv, f_send, f_recv, c_send, c_recv, r_send, r_recv, d_send, d_recv,
    out_send, out_recv, own_sem,
):
    me = lax.axis_index("tm")
    row = lax.axis_index("rows")
    left, right = (me + N - 1) % N, (me + 1) % N
    up, down = (row + 7) % 8, (row + 1) % 8

    def weight(i, w, wc, a):
        return pltpu.make_async_copy(
            w.at[pl.ds(a * 9 * C, 9 * C)], wc.at[:, pl.ds((2 - a) * C, C)], w_sem.at[i, a]
        )

    for i, (w, wc) in enumerate(((w1, wc1), (w2, wc2))):
        for a in range(3):
            weight(i, w, wc, a).start()

    barrier = pltpu.get_barrier_semaphore()
    for k in range(1, N):
        pl.semaphore_signal(barrier, inc=1, device_id=(peer(me, k), row), device_id_type=MESH)
    for dev in ((me, up), (me, down), (left, up), (left, down), (right, up), (right, down)):
        pl.semaphore_signal(barrier, inc=1, device_id=dev, device_id_type=MESH)

    nrm[:, 0:8] = jnp.zeros((H, 8, C), F32)
    nrm[:, 8 + COLS : 16 + COLS] = jnp.zeros((H, 8, C), F32)
    otr[...] = jnp.zeros_like(otr)

    def in_copy(q, k):
        return pltpu.make_async_remote_copy(
            src_ref=send.at[q, peer(me, k)],
            dst_ref=recv.at[q, me],
            send_sem=in_send.at[q, k],
            recv_sem=in_recv.at[q, k],
            device_id=(peer(me, k), row),
            device_id_type=MESH,
        )

    def in_arrival(q, k):
        return pltpu.make_async_remote_copy(
            src_ref=send.at[q, peer(me, k)],
            dst_ref=recv.at[q, source(me, k)],
            send_sem=in_send.at[q, k],
            recv_sem=in_recv.at[q, k],
            device_id=(peer(me, k), row),
            device_id_type=MESH,
        )

    gain1 = g1[...].reshape(1, C)
    for q in range(QI):

        def norm_row(r, _):
            nrm[r, 8 : 8 + COLS] = norm_act(lat[r].astype(F32), gain1)
            return 0

        lax.fori_loop(q * RI, (q + 1) * RI, norm_row, 0)
        for j in range(N):
            for r in range(RI):
                pk[j % 4, r * WH : (r + 1) * WH] = nrm[q * RI + r, j * W + 7 : j * W + 7 + WH]
            send[q, j] = pk[j % 4].astype(BF16)
        recv[q, me] = send[q, me]
        if q == 0:
            pl.semaphore_wait(barrier, N - 1 + 6)
        for k in ORDER:
            in_copy(q, k).start()

    def row_halo(i, ref, at, to, dev, s_sem, r_sem):
        return pltpu.make_async_remote_copy(
            src_ref=ref.at[at], dst_ref=ref.at[to], send_sem=s_sem.at[i], recv_sem=r_sem.at[i],
            device_id=dev, device_id_type=MESH,
        )

    field_up = row_halo(0, field, 1, H + 1, (me, up), f_send, f_recv)
    field_down = row_halo(1, field, H, 0, (me, down), f_send, f_recv)

    def arrive(q):
        for k in ORDER:
            in_arrival(q, k).wait_recv()

        def widen(f, _):
            v = recv[q, f].astype(F32)
            for lane in range(LANES):
                tr[lane, pl.ds(f * PI, PI)] = v[:, lane * 128 : (lane + 1) * 128]
            return 0

        lax.fori_loop(0, N, widen, 0)

        def turn(r, _):
            for c in range(WH):
                v = [tr[lane, pl.ds(r * WH + c, N, stride=PI)] for lane in range(LANES)]
                field[1 + q * RI + r, c] = jnp.concatenate(v, axis=-1).astype(BF16)
            return 0

        lax.fori_loop(0, RI, turn, 0)

    def multiply(src, wc, r0, rows):
        taps = [
            src[pl.ds(r0 + b, rows), e : e + W].reshape(rows * W * N, C)
            for b in range(3) for e in range(3)
        ]
        prod[0 : rows * W * N] = jnp.dot(
            jnp.concatenate(taps, axis=-1), wc[...], preferred_element_type=F32
        )

    def collect(px, count):
        v = prod[pl.ds(px * N, count * N)].reshape(count, N, 3 * C)
        return v[:, :, :C] + later(v[:, :, C : 2 * C], 1) + later(v[:, :, 2 * C :], 2)

    def first_rows(r0, rows):
        multiply(field, wc1, r0, rows)
        for r in range(rows):

            def finish(c, _):
                v = collect(r * W + c * 2, 2) + b1[...].reshape(1, C)
                second[r0 + r + 1, pl.ds(1 + c * 2, 2)] = norm_act(v, g2[...].reshape(1, C)).astype(BF16)
                return 0

            lax.fori_loop(0, W // 2, finish, 0)

    def side(i, r0, rows, which):
        src, dst, dev = ((1, W + 1, left), (W, 0, right))[which]
        return pltpu.make_async_remote_copy(
            src_ref=second.at[pl.ds(r0 + 1, rows), pl.ds(src, 1)],
            dst_ref=second.at[pl.ds(r0 + 1, rows), pl.ds(dst, 1)],
            send_sem=c_send.at[i, which], recv_sem=c_recv.at[i, which],
            device_id=(dev, row), device_id_type=MESH,
        )

    for a in range(3):
        weight(0, w1, wc1, a).wait()

    def pair(p, _):
        for q, first in ((0, 0), (1, 1), (2, 3)):

            @pl.when(p == first)
            def _():
                arrive(q)
                if q == 0:
                    field_up.start()
                if q == 2:
                    field_down.start()

        first_rows(1 + 2 * p, 2)
        side(p, 1 + 2 * p, 2, 0).start()
        side(p, 1 + 2 * p, 2, 1).start()
        return 0

    lax.fori_loop(0, PAIRS, pair, 0)

    edge = (
        (0, 0, H + 1, up),
        (H - 1, H + 1, 0, down),
    )

    def edge_copies(i):
        r, _, to, dev = edge[i]
        rows_copy = pltpu.make_async_remote_copy(
            src_ref=second.at[r + 1, pl.ds(1, W)], dst_ref=second.at[to, pl.ds(1, W)],
            send_sem=r_send.at[i], recv_sem=r_recv.at[i],
            device_id=(me, dev), device_id_type=MESH,
        )
        low = pltpu.make_async_remote_copy(
            src_ref=second.at[r + 1, pl.ds(1, 1)], dst_ref=second.at[to, pl.ds(W + 1, 1)],
            send_sem=d_send.at[i, 0], recv_sem=d_recv.at[i, 0],
            device_id=(left, dev), device_id_type=MESH,
        )
        high = pltpu.make_async_remote_copy(
            src_ref=second.at[r + 1, pl.ds(W, 1)], dst_ref=second.at[to, pl.ds(0, 1)],
            send_sem=d_send.at[i, 1], recv_sem=d_recv.at[i, 1],
            device_id=(right, dev), device_id_type=MESH,
        )
        return [rows_copy, low, high, side(PAIRS + i, r, 1, 0), side(PAIRS + i, r, 1, 1)]

    for i, arrival, missing in ((0, field_down, 0), (1, field_up, 7)):
        arrival.wait_recv()
        r, halo = edge[i][0], edge[i][1]

        @pl.when(row == missing)
        def _():
            field[halo] = jnp.zeros((WH, N, C), BF16)

        first_rows(r, 1)
        for copy in edge_copies(i):
            copy.start()

    for a in range(3):
        weight(1, w2, wc2, a).wait()

    def clear_sides(r0, rows):
        @pl.when(me == 0)
        def _():
            second[pl.ds(r0, rows), 0] = jnp.zeros((rows, N, C), BF16)

        @pl.when(me == N - 1)
        def _():
            second[pl.ds(r0, rows), W + 1] = jnp.zeros((rows, N, C), BF16)

    for p in range(PAIRS):
        for which in range(2):
            side(p, 1 + 2 * p, 2, which).wait_recv()
    clear_sides(2, H - 2)

    def out_copy(q, k):
        return pltpu.make_async_remote_copy(
            src_ref=ostage.at[q, peer(me, k)],
            dst_ref=out.at[me, q],
            send_sem=out_send.at[q, k],
            recv_sem=out_recv.at[q, k],
            device_id=(peer(me, k), row),
            device_id_type=MESH,
        )

    def out_arrival(q, k):
        return pltpu.make_async_remote_copy(
            src_ref=ostage.at[q, peer(me, k)],
            dst_ref=out.at[source(me, k), q],
            send_sem=out_send.at[q, k],
            recv_sem=out_recv.at[q, k],
            device_id=(peer(me, k), row),
            device_id_type=MESH,
        )

    def own_copy(q):
        return pltpu.make_async_copy(ostage.at[q, me], out.at[me, q], own_sem.at[q])

    def block(i, _):
        q = (i + 1) % QO

        @pl.when(i == 2)
        def _():
            for n in range(2):
                for copy in edge_copies(n):
                    copy.wait_recv()
            for n, missing in ((0, 7), (1, 0)):
                to = edge[n][2]

                @pl.when(row == missing)
                def _():
                    second[to] = jnp.zeros((WH, N, C), BF16)

            for r in (0, H):
                clear_sides(r, 2)

        multiply(second, wc2, q * RO, RO)

        def finish(px, _):
            v = collect(px, 1)[0] + b2[...].reshape(1, C)
            for lane in range(LANES):
                otr[lane, pl.ds(px, N, stride=PO)] = v[:, lane * 128 : (lane + 1) * 128]
            return 0

        lax.fori_loop(0, RO * W, finish, 0)

        def narrow(f, _):
            v = [otr[lane, pl.ds(f * PO, PO)] for lane in range(LANES)]
            ostage[q, f] = jnp.concatenate(v, axis=-1).astype(BF16)
            return 0

        lax.fori_loop(0, N, narrow, 0)
        for k in ORDER:
            out_copy(q, k).start()
        own_copy(q).start()
        return 0

    lax.fori_loop(0, QO, block, 0)

    for q in range(QO):
        for k in ORDER:
            out_arrival(q, k).wait_recv()
            out_copy(q, k).wait_send()
        own_copy(q).wait()
    for q in range(QI):
        for k in ORDER:
            in_copy(q, k).wait_send()
    field_up.wait_send()
    field_down.wait_send()
    for p in range(PAIRS):
        for which in range(2):
            side(p, 1 + 2 * p, 2, which).wait_send()
    for i in range(2):
        for copy in edge_copies(i):
            copy.wait_send()


def assemble(parts, lat, out, wide, line):
    for q in range(QO):
        for j in range(N):
            wide[j] = parts[j, q].astype(F32)
        for r in range(RO):
            for j in range(N):
                line[r, j * W : (j + 1) * W] = wide[j, r * W : (r + 1) * W]
            at = q * RO + r
            out[at] = (line[r] + lat[at].astype(F32)).astype(BF16)


def on_device(lat, g1, w1, b1, g2, w2, b2):
    lat = lat.reshape(H, COLS, C)
    vmem, hbm = pl.BlockSpec(memory_space=pltpu.VMEM), pl.BlockSpec(memory_space=pl.ANY)
    dma = pltpu.SemaphoreType.DMA
    parts = pl.pallas_call(
        kernel,
        out_shape=jax.ShapeDtypeStruct((N, QO, PO, C), BF16),
        in_specs=[vmem, vmem, hbm, vmem, vmem, hbm, vmem],
        out_specs=hbm,
        scratch_shapes=[
            pltpu.VMEM((9 * C, 3 * C), BF16),
            pltpu.VMEM((9 * C, 3 * C), BF16),
            pltpu.VMEM((H + 2, WH, N, C), BF16),
            pltpu.VMEM((H + 2, WH, N, C), BF16),
            pltpu.VMEM((QI, N, PI, C), BF16),
            pltpu.VMEM((QI, N, PI, C), BF16),
            pltpu.VMEM((H, COLS + 16, C), F32),
            pltpu.VMEM((4, PI, C), F32),
            pltpu.VMEM((LANES, N * PI, 128), F32),
            pltpu.VMEM((RO * W * N, 3 * C), F32),
            pltpu.VMEM((LANES, N * PO, 128), F32),
            pltpu.VMEM((QO, N, PO, C), BF16),
            dma((2, 3)),
            dma((QI, N)), dma((QI, N)),
            dma((2,)), dma((2,)),
            dma((PAIRS + 2, 2)), dma((PAIRS + 2, 2)),
            dma((2,)), dma((2,)),
            dma((2, 2)), dma((2, 2)),
            dma((QO, N)), dma((QO, N)),
            dma((QO,)),
        ],
        compiler_params=pltpu.CompilerParams(
            collective_id=0, has_side_effects=True, vmem_limit_bytes=60 << 20
        ),
        name="block",
    )(lat, g1, w1, b1, g2, w2, b2)
    result = pl.pallas_call(
        assemble,
        out_shape=jax.ShapeDtypeStruct((H, COLS, C), BF16),
        in_specs=[vmem, vmem],
        out_specs=vmem,
        scratch_shapes=[pltpu.VMEM((N, PO, C), F32), pltpu.VMEM((RO, COLS, C), F32)],
        compiler_params=pltpu.CompilerParams(vmem_limit_bytes=60 << 20),
        name="assemble",
    )(parts, lat)
    return result.reshape(1, H, COLS, C)


def solution(mesh):
    return jax.shard_map(
        on_device,
        mesh=mesh,
        in_specs=(P("tm", "rows", None, None), P(), P(), P(), P(), P(), P()),
        out_specs=P("tm", "rows", None, None),
        check_vma=False,
    )
```

time: 289 us -> 92.3 us (0.32)
  the two profiles are of different devices: /device:TPU:31 before, /device:TPU:1 now
where the time goes in v1:
time: 92.3 us; the launch traced here: 92.1 us
  Pallas kernels  92.1 us (100%)
    pallas_call x1, Pallas kernels, on_device(): pl.pallas_call(kernel, out_shape=jax.ShapeDtypeStruct((N, QO, PO, C), BF1...  88.2 us
    pallas_call x1, Pallas kernels, on_device(): pl.pallas_call(assemble, out_shape=jax.ShapeDtypeStruct((H, COLS, C), BF1...  3.85 us

profile of v1, /device:TPU:1, one launch (start us, length us, event | category | flops | bytes accessed | tf_op | source)
XLA Modules:
  0.0 92.1 jit_solution(8754124522869090502)
XLA Ops:
  0.0 88.2 %block.1.parts = bf16[16,4,32,384]{3,2,1,0:T(8,128)(2,1)} custom-call(bf16[12,160,384]{2,1,0:T(8,128)(2,1)} %bitcast.2, f32[384]{0:T(512)} %g1.1, bf16[10368,384]{1,0:T(8,128)(2,1)} %w1.1, f32[384]{0:T(512)} %b1.1, f32[384]{0:T(512)} %g2.1, bf16[10368,384]{1,0:T(8,128)(2,1)} %w2.1, f32[384]{0:T(512)} %b2.1), custom_call_target="tpu_custom_call" | custom-call | tf_op jit(solution)/shard_map/block/pallas_call | solution.py:355
  88.2 3.9 %assemble.1 = bf16[12,160,384]{2,1,0:T(8,128)(2,1)} custom-call(bf16[16,4,32,384]{3,2,1,0:T(8,128)(2,1)} %block.1.parts, bf16[12,160,384]{2,1,0:T(8,128)(2,1)} %bitcast.3), custom_call_target="tpu_custom_call" | custom-call | tf_op jit(solution)/shard_map/assemble/pallas_call | solution.py:387

commit v2 on v1

v2 whole, which is shorter than its diff:
```python
import functools

import jax
import jax.numpy as jnp
from jax import lax
from jax.experimental import pallas as pl
from jax.experimental.pallas import tpu as pltpu
from jax.sharding import PartitionSpec as P

MESH = pl.DeviceIdType.MESH
F32, BF16 = jnp.float32, jnp.bfloat16

C = 384
LANES = C // 128
H = 12
COLS = 160
N = 16
W = COLS // N
WH = W + 2
QI, RI = 3, 4
QO, RO = 4, 3
PI = RI * WH
PO = 32


def norm_act(v, gain):
    scale = lax.rsqrt(jnp.mean(v * v, axis=-1, keepdims=True) + 1e-06)
    u = v * scale * gain
    half = 0.5 * u
    return half + half * jnp.tanh(half)


def later(v, frames):
    at = lax.broadcasted_iota(jnp.int32, v.shape, v.ndim - 2)
    return jnp.where(at < frames, 0.0, pltpu.roll(v, frames, v.ndim - 2))


def peer(me, k):
    z, x, c = me // 8, (me // 2) % 4, me % 2
    dz, dx, dc = k // 8, (k // 2) % 4, k % 2
    return ((z + dz) % 2) * 8 + ((x + dx) % 4) * 2 + (c + dc) % 2


def source(me, k):
    z, x, c = me // 8, (me // 2) % 4, me % 2
    dz, dx, dc = k // 8, (k // 2) % 4, k % 2
    return ((z + dz) % 2) * 8 + ((x + 4 - dx) % 4) * 2 + (c + dc) % 2


ORDER = (12, 13, 4, 5, 10, 11, 14, 15, 2, 3, 6, 7, 8, 9, 1)


def kernel(
    lat_hbm, g1, w1, b1, g2, w2, b2,
    out,
    wc, act, recv, send, lat, nrm, pk, tr, prod, otr, ostage,
    w_sem, lat_sem, in_send, in_recv, f_send, f_recv, c_send, c_recv, r_send, r_recv,
    out_send, out_recv, own_sem,
):
    field, second = act.at[0], act.at[1]
    me = lax.axis_index("tm")
    row = lax.axis_index("rows")
    left, right = (me + N - 1) % N, (me + 1) % N
    up, down = (row + 7) % 8, (row + 1) % 8

    barrier = pltpu.get_barrier_semaphore()
    for dev in (up, down):
        pl.semaphore_signal(barrier, inc=1, device_id=(me, dev), device_id_type=MESH)
    for k in ORDER:
        pl.semaphore_signal(barrier, inc=1, device_id=(peer(me, k), row), device_id_type=MESH)

    lat_copy = pltpu.make_async_copy(lat_hbm, lat, lat_sem)
    lat_copy.start()

    def weight(i, a):
        return pltpu.make_async_copy(
            (w1, w2)[i].at[pl.ds(a * 9 * C, 9 * C)],
            wc.at[i, :, pl.ds((2 - a) * C, C)],
            w_sem.at[i, a],
        )

    for i in range(2):
        for a in range(3):
            weight(i, a).start()

    nrm[:, 0:8] = jnp.zeros((H, 8, C), F32)
    nrm[:, 8 + COLS : 16 + COLS] = jnp.zeros((H, 8, C), F32)
    otr[...] = jnp.zeros_like(otr)

    def in_copy(q, k):
        return pltpu.make_async_remote_copy(
            src_ref=send.at[q, peer(me, k)],
            dst_ref=recv.at[q, me],
            send_sem=in_send.at[q, k],
            recv_sem=in_recv.at[q, k],
            device_id=(peer(me, k), row),
            device_id_type=MESH,
        )

    def in_arrival(q, k):
        return pltpu.make_async_remote_copy(
            src_ref=send.at[q, peer(me, k)],
            dst_ref=recv.at[q, source(me, k)],
            send_sem=in_send.at[q, k],
            recv_sem=in_recv.at[q, k],
            device_id=(peer(me, k), row),
            device_id_type=MESH,
        )

    def norm_row(r, _):
        nrm[r, 8 : 8 + COLS] = norm_act(lat[r].astype(F32), g1[...].reshape(1, C))
        return 0

    def pack(q, _):
        for j in range(N):
            for n in range(RI):
                pk[j % 4, n * WH : (n + 1) * WH] = nrm[q * RI + n, j * W + 7 : j * W + 7 + WH]
            send[q, j] = pk[j % 4].astype(BF16)
        recv[q, me] = send[q, me]
        return 0

    def dispatch(q, _):
        for k in ORDER:
            in_copy(q, k).start()
        return 0

    lat_copy.wait()
    lax.fori_loop(0, H, norm_row, 0)
    lax.fori_loop(0, QI, pack, 0)
    pl.semaphore_wait(barrier, N - 1 + 2)
    lax.fori_loop(0, QI, dispatch, 0)

    def row_halo(i, ref, at, to, dev, columns, s_sem, r_sem):
        return pltpu.make_async_remote_copy(
            src_ref=ref.at[at, columns], dst_ref=ref.at[to, columns],
            send_sem=s_sem.at[i], recv_sem=r_sem.at[i],
            device_id=(me, dev), device_id_type=MESH,
        )

    every, own = pl.ds(0, WH), pl.ds(1, W)
    field_up = row_halo(0, field, 1, H + 1, up, every, f_send, f_recv)
    field_down = row_halo(1, field, H, 0, down, every, f_send, f_recv)

    def arrive(q):
        for k in ORDER:
            in_arrival(q, k).wait_recv()

        def widen(f, _):
            v = recv[q, f].astype(F32)
            for lane in range(LANES):
                tr[lane, pl.ds(f * PI, PI)] = v[:, lane * 128 : (lane + 1) * 128]
            return 0

        lax.fori_loop(0, N, widen, 0, unroll=4)
        for n in range(RI):

            def turn(c, _):
                v = [tr[lane, pl.ds(n * WH + c, N, stride=PI)] for lane in range(LANES)]
                field[1 + q * RI + n, c] = jnp.concatenate(v, axis=-1).astype(BF16)
                return 0

            lax.fori_loop(0, WH, turn, 0, unroll=True)

    def multiply(conv, rows):
        taps = [
            jnp.concatenate([act[conv, r + b, e : e + W] for r in rows], axis=0).reshape(-1, C)
            for b in range(3) for e in range(3)
        ]
        prod[...] = jnp.dot(
            jnp.concatenate(taps, axis=-1), wc[conv], preferred_element_type=F32
        )

    def collect(px, count):
        v = prod[pl.ds(px * N, count * N)].reshape(count, N, 3 * C)
        return v[:, :, :C] + later(v[:, :, C : 2 * C], 1) + later(v[:, :, 2 * C :], 2)

    def side(i, at, rows, which):
        src, dst, dev = ((1, W + 1, left), (W, 0, right))[which]
        return pltpu.make_async_remote_copy(
            src_ref=second.at[pl.ds(at, rows), pl.ds(src, 1)],
            dst_ref=second.at[pl.ds(at, rows), pl.ds(dst, 1)],
            send_sem=c_send.at[i, which], recv_sem=c_recv.at[i, which],
            device_id=(dev, row), device_id_type=MESH,
        )

    edges, halos = ((6, 1, 1), (7, H, 1)), ((8, 0, 1), (9, H + 1, 1))

    def start_sides(*which):
        for s in which:
            for n in range(2):
                side(*s, n).start()

    def await_sides(*which):
        for s in which:
            for n in range(2):
                side(*s, n).wait_recv()
            _, at, rows = s

            @pl.when(me == 0)
            def _():
                second[pl.ds(at, rows), 0] = jnp.zeros((rows, N, C), BF16)

            @pl.when(me == N - 1)
            def _():
                second[pl.ds(at, rows), W + 1] = jnp.zeros((rows, N, C), BF16)

    second_up = row_halo(0, second, 1, H + 1, up, own, r_send, r_recv)
    second_down = row_halo(1, second, H, 0, down, own, r_send, r_recv)

    def out_copy(q, k):
        return pltpu.make_async_remote_copy(
            src_ref=ostage.at[q, peer(me, k)],
            dst_ref=out.at[me, q],
            send_sem=out_send.at[q, k],
            recv_sem=out_recv.at[q, k],
            device_id=(peer(me, k), row),
            device_id_type=MESH,
        )

    def out_arrival(q, k):
        return pltpu.make_async_remote_copy(
            src_ref=ostage.at[q, peer(me, k)],
            dst_ref=out.at[source(me, k), q],
            send_sem=out_send.at[q, k],
            recv_sem=out_recv.at[q, k],
            device_id=(peer(me, k), row),
            device_id_type=MESH,
        )

    def own_copy(q):
        return pltpu.make_async_copy(ostage.at[q, me], out.at[me, q], own_sem.at[q])

    def finish_first(rows):
        for n, r in enumerate(rows):

            def some(g, _):
                v = collect(n * W + g * 2, 2) + b1[...].reshape(1, C)
                v = norm_act(v, g2[...].reshape(1, C))
                second[r + 1, pl.ds(1 + g * 2, 2)] = v.astype(BF16)
                return 0

            lax.fori_loop(0, W // 2, some, 0, unroll=True)

    def finish_second(rows):
        for n, r in enumerate(rows):

            def some(c, _):
                v = collect(n * W + c, 1)[0] + b2[...].reshape(1, C)
                px = (r // RO) * PO + (r % RO) * W + c
                for lane in range(LANES):
                    otr[lane, pl.ds(px, N, stride=QO * PO)] = v[:, lane * 128 : (lane + 1) * 128]
                return 0

            lax.fori_loop(0, W, some, 0, unroll=True)

    def give(q):
        def narrow(f, _):
            v = [otr[lane, pl.ds((f * QO + q) * PO, PO)] for lane in range(LANES)]
            ostage[q, f] = jnp.concatenate(v, axis=-1).astype(BF16)
            return 0

        lax.fori_loop(0, N, narrow, 0, unroll=4)
        for k in ORDER:
            out_copy(q, k).start()
        own_copy(q).start()

    def clear(ref, at, missing, low, high):
        @pl.when(row == missing)
        def _():
            ref[at, low:high] = jnp.zeros((high - low, N, C), BF16)

    def pair(i):
        return (i, 2 * i + 2, 2)

    def step(i, _):
        conv = jnp.where((i < 5) | (i == 6), 0, 1)

        @pl.when((i == 0) | (i == 1) | (i == 3))
        def _():
            arrive(i - i // 3)

        @pl.when(i == 0)
        def _():
            field_up.start()
            for a in range(3):
                weight(0, a).wait()

        @pl.when(i == 3)
        def _():
            field_down.start()

        @pl.when(i == 6)
        def _():
            field_down.wait_recv()
            clear(field, 0, 0, 0, WH)
            field_up.wait_recv()
            clear(field, H + 1, 7, 0, WH)

        @pl.when(i == 5)
        def _():
            for a in range(3):
                weight(1, a).wait()
            await_sides(pair(0), pair(1))

        @pl.when((i >= 7) & (i <= 9))
        def _():
            await_sides(pair(i - 5))

        @pl.when(i == 9)
        def _():
            second_down.wait_recv()
            clear(second, 0, 0, 1, 1 + W)
            second_up.wait_recv()
            clear(second, H + 1, 7, 1, 1 + W)
            start_sides(*halos)

        @pl.when(i == 10)
        def _():
            await_sides(edges[0], halos[0])

        @pl.when(i == 11)
        def _():
            await_sides(edges[1], halos[1])

        low = jnp.where(i < 5, 2 * i + 1, jnp.where(i == 5, 2, jnp.where(i == 11, 10, 2 * i - 10)))
        low = jnp.where((i == 6) | (i == 10), 0, low)
        high = jnp.where(i == 6, 11, low + 1)
        multiply(conv, (low, high))

        @pl.when(conv == 0)
        def _():
            finish_first((low, high))

        @pl.when(i == 6)
        def _():
            second_up.start()
            second_down.start()
            start_sides(*edges)

        @pl.when(i < 5)
        def _():
            start_sides(pair(i))

        @pl.when(conv == 1)
        def _():
            finish_second((low, high))

        @pl.when((i == 7) | (i >= 9))
        def _():
            give(jnp.where(i == 10, 0, (i - 5) // 2))

        return 0

    lax.fori_loop(0, 12, step, 0)

    def drain_in(q, _):
        for k in ORDER:
            in_copy(q, k).wait_send()
        return 0

    lax.fori_loop(0, QI, drain_in, 0)
    for copy in (field_up, field_down, second_up, second_down):
        copy.wait_send()
    for s in [pair(i) for i in range(5)] + list(edges + halos):
        for n in range(2):
            side(*s, n).wait_send()

    def drain_out(q, _):
        for k in ORDER:
            out_arrival(q, k).wait_recv()
            out_copy(q, k).wait_send()
        own_copy(q).wait()
        return 0

    lax.fori_loop(0, QO, drain_out, 0)


def assemble(parts, lat, out, wide, line):
    for j in range(N):
        wide[j] = parts[j, 0].astype(F32)
    for r in range(RO):
        for j in range(N):
            line[r, j * W : (j + 1) * W] = wide[j, r * W : (r + 1) * W]
        out[r] = (line[r] + lat[r].astype(F32)).astype(BF16)


def on_device(lat, g1, w1, b1, g2, w2, b2):
    lat = lat.reshape(H, COLS, C)
    vmem, hbm = pl.BlockSpec(memory_space=pltpu.VMEM), pl.BlockSpec(memory_space=pl.ANY)
    dma = pltpu.SemaphoreType.DMA
    parts = pl.pallas_call(
        kernel,
        out_shape=jax.ShapeDtypeStruct((N, QO, PO, C), BF16),
        in_specs=[hbm, vmem, hbm, vmem, vmem, hbm, vmem],
        out_specs=hbm,
        scratch_shapes=[
            pltpu.VMEM((2, 9 * C, 3 * C), BF16),
            pltpu.VMEM((2, H + 2, WH, N, C), BF16),
            pltpu.VMEM((QI, N, PI, C), BF16),
            pltpu.VMEM((QI, N, PI, C), BF16),
            pltpu.VMEM((H, COLS, C), BF16),
            pltpu.VMEM((H, COLS + 16, C), F32),
            pltpu.VMEM((4, PI, C), F32),
            pltpu.VMEM((LANES, N * PI, 128), F32),
            pltpu.VMEM((2 * W * N, 3 * C), F32),
            pltpu.VMEM((LANES, N * QO * PO, 128), F32),
            pltpu.VMEM((QO, N, PO, C), BF16),
            dma((2, 3)), dma,
            dma((QI, N)), dma((QI, N)),
            dma((2,)), dma((2,)),
            dma((10, 2)), dma((10, 2)),
            dma((2,)), dma((2,)),
            dma((QO, N)), dma((QO, N)),
            dma((QO,)),
        ],
        compiler_params=pltpu.CompilerParams(
            collective_id=0, has_side_effects=True, vmem_limit_bytes=60 << 20
        ),
        name="block",
    )(lat, g1, w1, b1, g2, w2, b2)
    result = pl.pallas_call(
        assemble,
        out_shape=jax.ShapeDtypeStruct((H, COLS, C), BF16),
        grid=(QO,),
        in_specs=[
            pl.BlockSpec((N, 1, PO, C), lambda q: (0, q, 0, 0)),
            pl.BlockSpec((RO, COLS, C), lambda q: (q, 0, 0)),
        ],
        out_specs=pl.BlockSpec((RO, COLS, C), lambda q: (q, 0, 0)),
        scratch_shapes=[pltpu.VMEM((N, PO, C), F32), pltpu.VMEM((RO, COLS, C), F32)],
        compiler_params=pltpu.CompilerParams(vmem_limit_bytes=32 << 20),
        name="assemble",
    )(parts, lat)
    return result.reshape(1, H, COLS, C)


def solution(mesh):
    return jax.shard_map(
        on_device,
        mesh=mesh,
        in_specs=(P("tm", "rows", None, None), P(), P(), P(), P(), P(), P()),
        out_specs=P("tm", "rows", None, None),
        check_vma=False,
    )
```

time: 92.3 us -> 90.2 us (0.977)
  Pallas kernels: 92.1 us -> 88.7 us
  local copies, waits for them, and re-layouts: 0 us -> 1.4 us
    pallas_call x1, Pallas kernels: 88.2 us -> 86.4 us  [on_device(): pl.pallas_call(kernel, out_shape=jax.ShapeDtypeStruct((N, QO, PO, C), BF1...]
    pallas_call x1, Pallas kernels: 3.85 us -> 2.3 us  [on_device(): pl.pallas_call(assemble, out_shape=jax.ShapeDtypeStruct((H, COLS, C), BF1...]
    unnamed x0 -> x4, local copies, waits for them, and re-layouts: none -> 1.4 us
where the time goes in v2:
time: 90.2 us; the launch traced here: 90.1 us
  Pallas kernels  88.7 us (98%)
  local copies, waits for them, and re-layouts  1.4 us (2%)
    pallas_call x1, Pallas kernels, on_device(): pl.pallas_call(kernel, out_shape=jax.ShapeDtypeStruct((N, QO, PO, C), BF1...  86.4 us
    pallas_call x1, Pallas kernels, on_device(): pl.pallas_call(assemble, out_shape=jax.ShapeDtypeStruct((H, COLS, C), BF1...  2.3 us

profile of v2, /device:TPU:1, one launch (start us, length us, event | category | flops | bytes accessed | tf_op | source)
XLA Modules:
  0.0 90.1 jit_solution(1353098772685359496)
XLA Ops:
  0.0 0.0 copy-start.1
  0.0 86.4 %block.1.parts = bf16[16,4,32,384]{3,2,1,0:T(8,128)(2,1)} custom-call(bf16[12,160,384]{2,1,0:T(8,128)(2,1)} %bitcast.2, f32[384]{0:T(512)} %g1.1, bf16[10368,384]{1,0:T(8,128)(2,1)} %w1.1, f32[384]{0:T(512)} %b1.1, f32[384]{0:T(512)} %g2.1, bf16[10368,384]{1,0:T(8,128)(2,1)} %w2.1, f32[384]{0:T(512)} %b2.1), custom_call_target="tpu_custom_call" | custom-call | tf_op jit(solution)/shard_map/block/pallas_call | solution.py:391
  86.4 0.0 copy-done.1
  86.4 0.0 copy-start
  86.4 1.4 %copy-done = bf16[16,4,32,384]{3,2,1,0:T(8,128)(2,1)S(1)} copy-done((bf16[16,4,32,384]{3,2,1,0:T(8,128)(2,1)S(1)}, bf16[16,4,32,384]{3,2,1,0:T(8,128)(2,1)}, u32[]{:S(2)}) %copy-start) | copy-done | bytes 1572888
  87.8 2.3 %assemble.1 = bf16[12,160,384]{2,1,0:T(8,128)(2,1)} custom-call(bf16[16,4,32,384]{3,2,1,0:T(8,128)(2,1)S(1)} %copy-done, bf16[12,160,384]{2,1,0:T(8,128)(2,1)S(1)} %bitcast.3), custom_call_target="tpu_custom_call" | custom-call | tf_op jit(solution)/shard_map/assemble/pallas_call | solution.py:421
Async XLA Ops:
  0.0 86.4 %copy-start.1 = (bf16[1,12,160,384]{3,2,1,0:T(8,128)(2,1)S(1)}, bf16[1,12,160,384]{3,2,1,0:T(8,128)(2,1)}, u32[]{:S(2)}) copy-start(bf16[1,12,160,384]{3,2,1,0:T(8,128)(2,1)} %param.7) | copy-start | bytes 4423684
  86.4 1.4 %copy-start = (bf16[16,4,32,384]{3,2,1,0:T(8,128)(2,1)S(1)}, bf16[16,4,32,384]{3,2,1,0:T(8,128)(2,1)}, u32[]{:S(2)}) copy-start(bf16[16,4,32,384]{3,2,1,0:T(8,128)(2,1)} %block.1.parts) | copy-start | bytes 4718596

commit v3 on v2

--- a/solution.py
+++ b/solution.py
@@ -19,6 +19,7 @@
 WH = W + 2
 QI, RI = 3, 4
 QO, RO = 4, 3
+OUT_FROM = 2
 PI = RI * WH
 PO = 32
 
@@ -54,7 +55,7 @@
     lat_hbm, g1, w1, b1, g2, w2, b2,
     out,
     wc, act, recv, send, lat, nrm, pk, tr, prod, otr, ostage,
-    w_sem, lat_sem, in_send, in_recv, f_send, f_recv, c_send, c_recv, r_send, r_recv,
+    w_sem, lat_sem, in_send, in_recv, f_send, f_recv, c_send, c_recv, r_send, r_recv, k_send, k_recv,
     out_send, out_recv, own_sem,
 ):
     field, second = act.at[0], act.at[1]
@@ -62,12 +63,14 @@
     row = lax.axis_index("rows")
     left, right = (me + N - 1) % N, (me + 1) % N
     up, down = (row + 7) % 8, (row + 1) % 8
+    to = {k: peer(me, k) for k in ORDER}
+    source_of = {k: source(me, k) for k in ORDER}
 
     barrier = pltpu.get_barrier_semaphore()
     for dev in (up, down):
         pl.semaphore_signal(barrier, inc=1, device_id=(me, dev), device_id_type=MESH)
     for k in ORDER:
-        pl.semaphore_signal(barrier, inc=1, device_id=(peer(me, k), row), device_id_type=MESH)
+        pl.semaphore_signal(barrier, inc=1, device_id=(to[k], row), device_id_type=MESH)
 
     lat_copy = pltpu.make_async_copy(lat_hbm, lat, lat_sem)
     lat_copy.start()
@@ -89,21 +92,21 @@
 
     def in_copy(q, k):
         return pltpu.make_async_remote_copy(
-            src_ref=send.at[q, peer(me, k)],
+            src_ref=send.at[q, to[k]],
             dst_ref=recv.at[q, me],
             send_sem=in_send.at[q, k],
             recv_sem=in_recv.at[q, k],
-            device_id=(peer(me, k), row),
+            device_id=(to[k], row),
             device_id_type=MESH,
         )
 
     def in_arrival(q, k):
         return pltpu.make_async_remote_copy(
-            src_ref=send.at[q, peer(me, k)],
-            dst_ref=recv.at[q, source(me, k)],
+            src_ref=send.at[q, to[k]],
+            dst_ref=recv.at[q, source_of[k]],
             send_sem=in_send.at[q, k],
             recv_sem=in_recv.at[q, k],
-            device_id=(peer(me, k), row),
+            device_id=(to[k], row),
             device_id_type=MESH,
         )
 
@@ -130,9 +133,9 @@
     pl.semaphore_wait(barrier, N - 1 + 2)
     lax.fori_loop(0, QI, dispatch, 0)
 
-    def row_halo(i, ref, at, to, dev, columns, s_sem, r_sem):
-        return pltpu.make_async_remote_copy(
-            src_ref=ref.at[at, columns], dst_ref=ref.at[to, columns],
+    def row_halo(i, ref, at, target, dev, columns, s_sem, r_sem):
+        return pltpu.make_async_remote_copy(
+            src_ref=ref.at[at, columns], dst_ref=ref.at[target, columns],
             send_sem=s_sem.at[i], recv_sem=r_sem.at[i],
             device_id=(me, dev), device_id_type=MESH,
         )
@@ -183,7 +186,10 @@
             device_id=(dev, row), device_id_type=MESH,
         )
 
-    edges, halos = ((6, 1, 1), (7, H, 1)), ((8, 0, 1), (9, H + 1, 1))
+    edges = ((5, 1, 1), (6, H, 1))
+
+    def pair(p):
+        return (p, 2 * p + 2, 2)
 
     def start_sides(*which):
         for s in which:
@@ -204,26 +210,33 @@
             def _():
                 second[pl.ds(at, rows), W + 1] = jnp.zeros((rows, N, C), BF16)
 
+    corners = []
+    for i, (at, target, dev) in enumerate(((1, H + 1, up), (H, 0, down))):
+        corners.append([
+            row_halo(n, second, at, target, dev, pl.ds(column, 1), k_send.at[i], k_recv.at[i])
+            for n, column in enumerate((0, W + 1))
+        ])
+
     second_up = row_halo(0, second, 1, H + 1, up, own, r_send, r_recv)
     second_down = row_halo(1, second, H, 0, down, own, r_send, r_recv)
 
     def out_copy(q, k):
         return pltpu.make_async_remote_copy(
-            src_ref=ostage.at[q, peer(me, k)],
+            src_ref=ostage.at[q, to[k]],
             dst_ref=out.at[me, q],
             send_sem=out_send.at[q, k],
             recv_sem=out_recv.at[q, k],
-            device_id=(peer(me, k), row),
+            device_id=(to[k], row),
             device_id_type=MESH,
         )
 
     def out_arrival(q, k):
         return pltpu.make_async_remote_copy(
-            src_ref=ostage.at[q, peer(me, k)],
-            dst_ref=out.at[source(me, k), q],
+            src_ref=ostage.at[q, to[k]],
+            dst_ref=out.at[source_of[k], q],
             send_sem=out_send.at[q, k],
             recv_sem=out_recv.at[q, k],
-            device_id=(peer(me, k), row),
+            device_id=(to[k], row),
             device_id_type=MESH,
         )
 
@@ -246,7 +259,8 @@
 
             def some(c, _):
                 v = collect(n * W + c, 1)[0] + b2[...].reshape(1, C)
-                px = (r // RO) * PO + (r % RO) * W + c
+                slot = (r + H - OUT_FROM) % H
+                px = (slot // RO) * PO + (slot % RO) * W + c
                 for lane in range(LANES):
                     otr[lane, pl.ds(px, N, stride=QO * PO)] = v[:, lane * 128 : (lane + 1) * 128]
                 return 0
@@ -264,16 +278,21 @@
             out_copy(q, k).start()
         own_copy(q).start()
 
-    def clear(ref, at, missing, low, high):
+    def clear(ref, at, missing):
         @pl.when(row == missing)
         def _():
-            ref[at, low:high] = jnp.zeros((high - low, N, C), BF16)
-
-    def pair(i):
-        return (i, 2 * i + 2, 2)
+            ref[at] = jnp.zeros((WH, N, C), BF16)
+
+    def table(i, values):
+        value = values[0]
+        for n in range(1, len(values)):
+            value = jnp.where(i == n, values[n], value)
+        return value
 
     def step(i, _):
-        conv = jnp.where((i < 5) | (i == 6), 0, 1)
+        conv = table(i, (0, 0, 0, 0, 0, 1, 0, 1, 1, 1, 1, 1))
+        low = table(i, (1, 3, 5, 7, 9, 2, 0, 4, 6, 8, 1, 0))
+        high = table(i, (2, 4, 6, 8, 10, 3, 11, 5, 7, 9, 10, 11))
 
         @pl.when((i == 0) | (i == 1) | (i == 3))
         def _():
@@ -281,20 +300,13 @@
 
         @pl.when(i == 0)
         def _():
-            field_up.start()
             for a in range(3):
                 weight(0, a).wait()
 
         @pl.when(i == 3)
         def _():
             field_down.start()
-
-        @pl.when(i == 6)
-        def _():
-            field_down.wait_recv()
-            clear(field, 0, 0, 0, WH)
-            field_up.wait_recv()
-            clear(field, H + 1, 7, 0, WH)
+            field_up.start()
 
         @pl.when(i == 5)
         def _():
@@ -302,29 +314,24 @@
                 weight(1, a).wait()
             await_sides(pair(0), pair(1))
 
+        @pl.when(i == 6)
+        def _():
+            field_down.wait_recv()
+            clear(field, 0, 0)
+            field_up.wait_recv()
+            clear(field, H + 1, 7)
+
         @pl.when((i >= 7) & (i <= 9))
         def _():
             await_sides(pair(i - 5))
 
-        @pl.when(i == 9)
-        def _():
-            second_down.wait_recv()
-            clear(second, 0, 0, 1, 1 + W)
-            second_up.wait_recv()
-            clear(second, H + 1, 7, 1, 1 + W)
-            start_sides(*halos)
-
-        @pl.when(i == 10)
-        def _():
-            await_sides(edges[0], halos[0])
-
         @pl.when(i == 11)
         def _():
-            await_sides(edges[1], halos[1])
-
-        low = jnp.where(i < 5, 2 * i + 1, jnp.where(i == 5, 2, jnp.where(i == 11, 10, 2 * i - 10)))
-        low = jnp.where((i == 6) | (i == 10), 0, low)
-        high = jnp.where(i == 6, 11, low + 1)
+            for copy in [second_down, second_up] + corners[0] + corners[1]:
+                copy.wait_recv()
+            clear(second, 0, 0)
+            clear(second, H + 1, 7)
+
         multiply(conv, (low, high))
 
         @pl.when(conv == 0)
@@ -341,13 +348,19 @@
         def _():
             start_sides(pair(i))
 
+        @pl.when(i == 8)
+        def _():
+            await_sides(*edges)
+            for copy in corners[0] + corners[1]:
+                copy.start()
+
         @pl.when(conv == 1)
         def _():
             finish_second((low, high))
 
-        @pl.when((i == 7) | (i >= 9))
-        def _():
-            give(jnp.where(i == 10, 0, (i - 5) // 2))
+        @pl.when((i == 7) | (i == 8) | (i >= 10))
+        def _():
+            give(i - 7 - i // 10)
 
         return 0
 
@@ -359,9 +372,9 @@
         return 0
 
     lax.fori_loop(0, QI, drain_in, 0)
-    for copy in (field_up, field_down, second_up, second_down):
+    for copy in [field_up, field_down, second_up, second_down] + corners[0] + corners[1]:
         copy.wait_send()
-    for s in [pair(i) for i in range(5)] + list(edges + halos):
+    for s in [pair(p) for p in range(5)] + list(edges):
         for n in range(2):
             side(*s, n).wait_send()
 
@@ -376,12 +389,14 @@
 
 
 def assemble(parts, lat, out, wide, line):
+    q = pl.program_id(0)
     for j in range(N):
         wide[j] = parts[j, 0].astype(F32)
     for r in range(RO):
         for j in range(N):
             line[r, j * W : (j + 1) * W] = wide[j, r * W : (r + 1) * W]
-        out[r] = (line[r] + lat[r].astype(F32)).astype(BF16)
+        at = (q * RO + r + OUT_FROM) % H
+        out[at] = (line[r] + lat[at].astype(F32)).astype(BF16)
 
 
 def on_device(lat, g1, w1, b1, g2, w2, b2):
@@ -408,8 +423,9 @@
             dma((2, 3)), dma,
             dma((QI, N)), dma((QI, N)),
             dma((2,)), dma((2,)),
-            dma((10, 2)), dma((10, 2)),
+            dma((7, 2)), dma((7, 2)),
             dma((2,)), dma((2,)),
+            dma((2, 2)), dma((2, 2)),
             dma((QO, N)), dma((QO, N)),
             dma((QO,)),
         ],
@@ -424,9 +440,9 @@
         grid=(QO,),
         in_specs=[
             pl.BlockSpec((N, 1, PO, C), lambda q: (0, q, 0, 0)),
-            pl.BlockSpec((RO, COLS, C), lambda q: (q, 0, 0)),
+            pl.BlockSpec((H, COLS, C), lambda q: (0, 0, 0)),
         ],
-        out_specs=pl.BlockSpec((RO, COLS, C), lambda q: (q, 0, 0)),
+        out_specs=pl.BlockSpec((H, COLS, C), lambda q: (0, 0, 0)),
         scratch_shapes=[pltpu.VMEM((N, PO, C), F32), pltpu.VMEM((RO, COLS, C), F32)],
         compiler_params=pltpu.CompilerParams(vmem_limit_bytes=32 << 20),
         name="assemble",

time: 90.2 us -> 85.6 us (0.949)
  Pallas kernels: 88.7 us -> 84 us
    pallas_call x1, Pallas kernels: 86.4 us -> 81.8 us  [on_device(): pl.pallas_call(kernel, out_shape=jax.ShapeDtypeStruct((N, QO, PO, C), BF1...]
where the time goes in v3:
time: 85.6 us; the launch traced here: 85.4 us
  Pallas kernels  84 us (98%)
  local copies, waits for them, and re-layouts  1.4 us (2%)
    pallas_call x1, Pallas kernels, on_device(): pl.pallas_call(kernel, out_shape=jax.ShapeDtypeStruct((N, QO, PO, C), BF1...  81.8 us
    pallas_call x1, Pallas kernels, on_device(): pl.pallas_call(assemble, out_shape=jax.ShapeDtypeStruct((H, COLS, C), BF1...  2.21 us

profile of v3, /device:TPU:1, one launch (start us, length us, event | category | flops | bytes accessed | tf_op | source)
XLA Modules:
  0.0 85.4 jit_solution(3203532709757063188)
XLA Ops:
  0.0 0.0 copy-start.1
  0.0 81.8 %block.1.parts = bf16[16,4,32,384]{3,2,1,0:T(8,128)(2,1)} custom-call(bf16[12,160,384]{2,1,0:T(8,128)(2,1)} %bitcast.2, f32[384]{0:T(512)} %g1.1, bf16[10368,384]{1,0:T(8,128)(2,1)} %w1.1, f32[384]{0:T(512)} %b1.1, f32[384]{0:T(512)} %g2.1, bf16[10368,384]{1,0:T(8,128)(2,1)} %w2.1, f32[384]{0:T(512)} %b2.1), custom_call_target="tpu_custom_call" | custom-call | tf_op jit(solution)/shard_map/block/pallas_call | solution.py:406
  81.8 0.0 copy-done.1
  81.8 0.0 copy-start
  81.8 1.4 %copy-done = bf16[16,4,32,384]{3,2,1,0:T(8,128)(2,1)S(1)} copy-done((bf16[16,4,32,384]{3,2,1,0:T(8,128)(2,1)S(1)}, bf16[16,4,32,384]{3,2,1,0:T(8,128)(2,1)}, u32[]{:S(2)}) %copy-start) | copy-done | bytes 1572888
  83.2 2.2 %assemble.1 = bf16[12,160,384]{2,1,0:T(8,128)(2,1)} custom-call(bf16[16,4,32,384]{3,2,1,0:T(8,128)(2,1)S(1)} %copy-done, bf16[12,160,384]{2,1,0:T(8,128)(2,1)S(1)} %bitcast.3), custom_call_target="tpu_custom_call" | custom-call | tf_op jit(solution)/shard_map/assemble/pallas_call | solution.py:437
Async XLA Ops:
  0.0 81.8 %copy-start.1 = (bf16[1,12,160,384]{3,2,1,0:T(8,128)(2,1)S(1)}, bf16[1,12,160,384]{3,2,1,0:T(8,128)(2,1)}, u32[]{:S(2)}) copy-start(bf16[1,12,160,384]{3,2,1,0:T(8,128)(2,1)} %param.7) | copy-start | bytes 4423684
  81.8 1.4 %copy-start = (bf16[16,4,32,384]{3,2,1,0:T(8,128)(2,1)S(1)}, bf16[16,4,32,384]{3,2,1,0:T(8,128)(2,1)}, u32[]{:S(2)}) copy-start(bf16[16,4,32,384]{3,2,1,0:T(8,128)(2,1)} %block.1.parts) | copy-start | bytes 4718596

commit v4 on v3

--- a/solution.py
+++ b/solution.py
@@ -128,10 +128,19 @@
         return 0
 
     lat_copy.wait()
-    lax.fori_loop(0, H, norm_row, 0)
-    lax.fori_loop(0, QI, pack, 0)
+    def ready(q, _):
+        lax.fori_loop(q * RI, (q + 1) * RI, norm_row, 0)
+        return pack(q, 0)
+
+    ready(0, 0)
     pl.semaphore_wait(barrier, N - 1 + 2)
-    lax.fori_loop(0, QI, dispatch, 0)
+    dispatch(0, 0)
+
+    def follow(q, _):
+        ready(q, 0)
+        return dispatch(q, 0)
+
+    lax.fori_loop(1, QI, follow, 0)
 
     def row_halo(i, ref, at, target, dev, columns, s_sem, r_sem):
         return pltpu.make_async_remote_copy(
@@ -155,7 +164,7 @@
             return 0
 
         lax.fori_loop(0, N, widen, 0, unroll=4)
-        for n in range(RI):
+        for n in (3, 0, 1, 2):
 
             def turn(c, _):
                 v = [tr[lane, pl.ds(n * WH + c, N, stride=PI)] for lane in range(LANES)]
@@ -163,6 +172,13 @@
                 return 0
 
             lax.fori_loop(0, WH, turn, 0, unroll=True)
+            if n == 3:
+
+                @pl.when(q == QI - 1)
+                def _():
+                    field_down.start()
+                    field_up.start()
+
 
     def multiply(conv, rows):
         taps = [
@@ -303,11 +319,6 @@
             for a in range(3):
                 weight(0, a).wait()
 
-        @pl.when(i == 3)
-        def _():
-            field_down.start()
-            field_up.start()
-
         @pl.when(i == 5)
         def _():
             for a in range(3):
@@ -358,9 +369,9 @@
         def _():
             finish_second((low, high))
 
-        @pl.when((i == 7) | (i == 8) | (i >= 10))
-        def _():
-            give(i - 7 - i // 10)
+        @pl.when(i >= 8)
+        def _():
+            give(i - 8)
 
         return 0
 

time: 85.6 us -> 82.1 us (0.959)
  Pallas kernels: 84 us -> 80.5 us
    pallas_call x1, Pallas kernels: 81.8 us -> 78.3 us  [on_device(): pl.pallas_call(kernel, out_shape=jax.ShapeDtypeStruct((N, QO, PO, C), BF1...]
where the time goes in v4:
time: 82.1 us; the launch traced here: 81.9 us
  Pallas kernels  80.5 us (98%)
  local copies, waits for them, and re-layouts  1.4 us (2%)
    pallas_call x1, Pallas kernels, on_device(): pl.pallas_call(kernel, out_shape=jax.ShapeDtypeStruct((N, QO, PO, C), BF1...  78.3 us
    pallas_call x1, Pallas kernels, on_device(): pl.pallas_call(assemble, out_shape=jax.ShapeDtypeStruct((H, COLS, C), BF1...  2.21 us

profile of v4, /device:TPU:1, one launch (start us, length us, event | category | flops | bytes accessed | tf_op | source)
XLA Modules:
  0.0 81.9 jit_solution(11054744264517645332)
XLA Ops:
  0.0 0.0 copy-start.1
  0.0 78.3 %block.1.parts = bf16[16,4,32,384]{3,2,1,0:T(8,128)(2,1)} custom-call(bf16[12,160,384]{2,1,0:T(8,128)(2,1)} %bitcast.2, f32[384]{0:T(512)} %g1.1, bf16[10368,384]{1,0:T(8,128)(2,1)} %w1.1, f32[384]{0:T(512)} %b1.1, f32[384]{0:T(512)} %g2.1, bf16[10368,384]{1,0:T(8,128)(2,1)} %w2.1, f32[384]{0:T(512)} %b2.1), custom_call_target="tpu_custom_call" | custom-call | tf_op jit(solution)/shard_map/block/pallas_call | solution.py:417
  78.3 0.0 copy-done.1
  78.3 0.0 copy-start
  78.3 1.4 %copy-done = bf16[16,4,32,384]{3,2,1,0:T(8,128)(2,1)S(1)} copy-done((bf16[16,4,32,384]{3,2,1,0:T(8,128)(2,1)S(1)}, bf16[16,4,32,384]{3,2,1,0:T(8,128)(2,1)}, u32[]{:S(2)}) %copy-start) | copy-done | bytes 1572888
  79.7 2.2 %assemble.1 = bf16[12,160,384]{2,1,0:T(8,128)(2,1)} custom-call(bf16[16,4,32,384]{3,2,1,0:T(8,128)(2,1)S(1)} %copy-done, bf16[12,160,384]{2,1,0:T(8,128)(2,1)S(1)} %bitcast.3), custom_call_target="tpu_custom_call" | custom-call | tf_op jit(solution)/shard_map/assemble/pallas_call | solution.py:448
Async XLA Ops:
  0.0 78.3 %copy-start.1 = (bf16[1,12,160,384]{3,2,1,0:T(8,128)(2,1)S(1)}, bf16[1,12,160,384]{3,2,1,0:T(8,128)(2,1)}, u32[]{:S(2)}) copy-start(bf16[1,12,160,384]{3,2,1,0:T(8,128)(2,1)} %param.7) | copy-start | bytes 4423684
  78.3 1.4 %copy-start = (bf16[16,4,32,384]{3,2,1,0:T(8,128)(2,1)S(1)}, bf16[16,4,32,384]{3,2,1,0:T(8,128)(2,1)}, u32[]{:S(2)}) copy-start(bf16[16,4,32,384]{3,2,1,0:T(8,128)(2,1)} %block.1.parts) | copy-start | bytes 4718596

commit v5 on v4

--- a/solution.py
+++ b/solution.py
@@ -359,7 +359,7 @@
         def _():
             start_sides(pair(i))
 
-        @pl.when(i == 8)
+        @pl.when(i == 7)
         def _():
             await_sides(*edges)
             for copy in corners[0] + corners[1]:

time: 82.1 us -> 82.1 us (level)
  no operation moved by 1% of the time
where the time goes in v5:
time: 82.1 us; the launch traced here: 81.9 us
  Pallas kernels  80.5 us (98%)
  local copies, waits for them, and re-layouts  1.4 us (2%)
    pallas_call x1, Pallas kernels, on_device(): pl.pallas_call(kernel, out_shape=jax.ShapeDtypeStruct((N, QO, PO, C), BF1...  78.3 us
    pallas_call x1, Pallas kernels, on_device(): pl.pallas_call(assemble, out_shape=jax.ShapeDtypeStruct((H, COLS, C), BF1...  2.21 us

profile of v5, /device:TPU:1, one launch (start us, length us, event | category | flops | bytes accessed | tf_op | source)
XLA Modules:
  0.0 81.9 jit_solution(13878550779304051314)
XLA Ops:
  0.0 0.0 copy-start.1
  0.0 78.3 %block.1.parts = bf16[16,4,32,384]{3,2,1,0:T(8,128)(2,1)} custom-call(bf16[12,160,384]{2,1,0:T(8,128)(2,1)} %bitcast.2, f32[384]{0:T(512)} %g1.1, bf16[10368,384]{1,0:T(8,128)(2,1)} %w1.1, f32[384]{0:T(512)} %b1.1, f32[384]{0:T(512)} %g2.1, bf16[10368,384]{1,0:T(8,128)(2,1)} %w2.1, f32[384]{0:T(512)} %b2.1), custom_call_target="tpu_custom_call" | custom-call | tf_op jit(solution)/shard_map/block/pallas_call | solution.py:417
  78.3 0.0 copy-done.1
  78.3 0.0 copy-start
  78.3 1.4 %copy-done = bf16[16,4,32,384]{3,2,1,0:T(8,128)(2,1)S(1)} copy-done((bf16[16,4,32,384]{3,2,1,0:T(8,128)(2,1)S(1)}, bf16[16,4,32,384]{3,2,1,0:T(8,128)(2,1)}, u32[]{:S(2)}) %copy-start) | copy-done | bytes 1572888
  79.7 2.2 %assemble.1 = bf16[12,160,384]{2,1,0:T(8,128)(2,1)} custom-call(bf16[16,4,32,384]{3,2,1,0:T(8,128)(2,1)S(1)} %copy-done, bf16[12,160,384]{2,1,0:T(8,128)(2,1)S(1)} %bitcast.3), custom_call_target="tpu_custom_call" | custom-call | tf_op jit(solution)/shard_map/assemble/pallas_call | solution.py:448
Async XLA Ops:
  0.0 78.3 %copy-start.1 = (bf16[1,12,160,384]{3,2,1,0:T(8,128)(2,1)S(1)}, bf16[1,12,160,384]{3,2,1,0:T(8,128)(2,1)}, u32[]{:S(2)}) copy-start(bf16[1,12,160,384]{3,2,1,0:T(8,128)(2,1)} %param.7) | copy-start | bytes 4423684
  78.3 1.4 %copy-start = (bf16[16,4,32,384]{3,2,1,0:T(8,128)(2,1)S(1)}, bf16[16,4,32,384]{3,2,1,0:T(8,128)(2,1)}, u32[]{:S(2)}) copy-start(bf16[16,4,32,384]{3,2,1,0:T(8,128)(2,1)} %block.1.parts) | copy-start | bytes 4718596
